TPU v7x, 256 devices: a whole 4x4x8 slice. The times are simulated.
256 devices in a mesh: dp: 32 (over x_hi, z, core), tensor: 8 (over y, x_lo).
Axes of the slice: x: 4 (x_hi: 2, x_lo: 2; x = x_hi * 2 + x_lo), y: 4, z: 8, core: 2. Of those that a mesh axis runs over, the one named last changes fastest.
Arguments:
- grads: bfloat16 [32, 8192, 2, 1024], P('dp', None, None, 'tensor'), may hold values from -41 to 41
- errors: bfloat16 [32, 8192, 2, 1024], P('dp', None, None, 'tensor'), may hold values from -1.1953125 to 1.1953125
- q_prev: float32 [2, 1024, 64], P(None, 'tensor'), may hold values from -6 to 6
Outputs:
- new_errors: bfloat16 [32, 8192, 2, 1024], P('dp', None, None, 'tensor')
- p_factors: bfloat16 [2, 8192, 64], P(None, 'dp')
- q_factors: float32 [2, 1024, 64], P(None, 'tensor')
All inputs are finite; a program needn't handle non-finite values.
Results may differ from a plain program's by a relative error of at most 0.001.
Values sent between devices are 32-bit elements; how exact they have to be, the bound alone decides.
No kernel may reach another device: no remote copies, remote signals or barrier semaphores. Data moves between devices by JAX's collectives and lax.ppermute only.
A program may use at most 128 MiB of HBM per device.

v0:
```python
import functools

import jax
import jax.numpy as jnp
from jax import lax
from jax.experimental import pallas as pl
from jax.experimental.pallas import tpu as pltpu
from jax.sharding import Mesh
from jax.sharding import PartitionSpec as P

D = 8192
KVW = 1024
R = 64
REPLICAS = 32
F32 = jnp.float32
BF16 = jnp.bfloat16

AXES = ("x_hi", "z", "core", "y", "x_lo")
REPLICA = ("x_hi", "z", "core")
TENSOR = ("y", "x_lo")
BLOCK = ("core", "y", "x_lo")

BLOCKS = 16
ROWS = 256
LOADS = (8, 8)
AHEAD = 2
STEP = 4
SEND = 2
PANEL = 8
LIMIT = 16 * 1024 * 1024


def chip_groups():
    def device(x, z, core, y):
        return (((x // 2 * 8 + z) * 2 + core) * 4 + y) * 2 + x % 2

    def line(core, along, across, z):
        x, y = (along, across) if core == 0 else (across, along)
        return device(x, z, core, y)

    near, far = [], []
    for core in range(2):
        pairs = [((2 * k + core) % 8, (2 * k + core + 1) % 8) for k in range(4)]
        for across in range(4):
            for pair in pairs:
                near.append([line(core, i, across, z) for z in pair for i in range(4)])
            for which in range(2):
                far.append([line(core, across, i, p[which]) for p in pairs for i in range(4)])
    return near, far


NEAR, FAR = chip_groups()


WAYS = ((1, 0), (0, 1), (0, 3), (0, 2), (1, 1), (1, 3), (1, 2))


def way_pairs(flip, shift):
    pairs = []
    for group in NEAR:
        for at in range(8):
            there = (at // 4 ^ flip) * 4 + (at + shift) % 4
            pairs.append((group[at], group[there]))
    return pairs


def exchange(pieces, groups):
    return lax.all_to_all(pieces, AXES, 0, 0, axis_index_groups=groups, tiled=True)


def in_hbm(value):
    return pltpu.with_memory_space_constraint(value, pltpu.HBM)


def split(value):
    high = value.astype(BF16)
    low = (value - high.astype(F32)).astype(BF16)
    return high, low


def split_dot(a, b, a_dim, b_dim):
    line = jnp.concatenate(split(b), 1 - b_dim)
    both = lax.dot_general(
        jnp.concatenate(split(a), a_dim),
        jnp.concatenate([line, line], b_dim),
        (((a_dim,), (b_dim,)), ((), ())),
        preferred_element_type=F32,
    )
    n = both.shape[1] // 2
    return both[:, :n] + both[:, n:]


def first_projection(shape):
    return lax.broadcasted_iota(jnp.int32, shape, len(shape) - 1) < R


VMEM = pl.BlockSpec(memory_space=pltpu.VMEM)
ANY = pl.BlockSpec(memory_space=pl.ANY)
HALF_P = (BLOCKS, ROWS, 128)
HALF_X = (BLOCKS, 2 * ROWS, 128)
HALF_S = (BLOCKS, 2 * ROWS, 256)


def in_vmem(value):
    return pltpu.with_memory_space_constraint(value, pltpu.VMEM)


def left_kernel(mine, g_hbm, e_hbm, qt_hbm, p_ref, g_ref, e_ref, qt, weights, rows, arrived, qt_arrived):
    core = lax.axis_index("core")
    half = core if mine else 1 - core
    qt_copy = pltpu.make_async_copy(qt_hbm, qt, qt_arrived)
    qt_copy.start()
    copies = []
    for c, count in enumerate(LOADS):
        blocks = pl.ds(sum(LOADS[:c]), count)
        pair = (
            pltpu.make_async_copy(g_hbm.at[half, blocks], g_ref.at[blocks], arrived.at[0, c]),
            pltpu.make_async_copy(e_hbm.at[half, blocks], e_ref.at[blocks], arrived.at[1, c]),
        )
        copies.append(pair)
    for pair in copies[:AHEAD]:
        for copy in pair:
            copy.start(priority=1)
    qt_copy.wait()
    high, low = split(qt[...])
    weights[...] = jnp.concatenate(
        [jnp.concatenate([high, high], 1), jnp.concatenate([low, low], 1)], 0
    )
    mask = first_projection((ROWS, 2 * R))
    for c, pair in enumerate(copies):
        for copy in pair:
            copy.wait()
        for copy in copies[c + AHEAD] if c + AHEAD < len(copies) else ():
            copy.start(priority=1)
        for block in range(sum(LOADS[:c]), sum(LOADS[: c + 1])):
            x = jnp.concatenate([g_ref[block], e_ref[block]], 1)
            both = lax.dot_general(
                x, weights[...], (((1,), (1,)), ((), ())), preferred_element_type=F32
            )
            slot = rows.at[block % STEP]
            slot[...] = both[:, : 2 * R] + both[:, 2 * R :]
            even = slot[pl.ds(0, ROWS, stride=2), :]
            odd = slot[pl.ds(1, ROWS, stride=2), :]
            p_ref[block] = jnp.where(mask, even, odd)


def left_half(mine, g, e, qt):
    return pl.pallas_call(
        functools.partial(left_kernel, mine),
        in_specs=[ANY, ANY, ANY],
        out_specs=[VMEM, VMEM, VMEM],
        out_shape=[
            pltpu.VMEM(HALF_P, F32),
            pltpu.VMEM(HALF_X, BF16),
            pltpu.VMEM(HALF_X, BF16),
        ],
        scratch_shapes=[
            pltpu.VMEM((2 * R, 128), F32),
            pltpu.VMEM((256, 256), BF16),
            pltpu.VMEM((STEP, 2 * ROWS, 128), F32),
            pltpu.SemaphoreType.DMA((2, len(LOADS))),
            pltpu.SemaphoreType.DMA,
        ],
        compiler_params=pltpu.CompilerParams(vmem_limit_bytes=LIMIT),
        cost_estimate=pl.CostEstimate(
            flops=2 * 8192 * 256 * 256, bytes_accessed=8 * 2**20, transcendentals=0
        ),
        name="left_half",
    )(in_hbm(g), in_hbm(e), in_hbm(qt))


def interleave(p, rows, mask):
    rows[pl.ds(0, ROWS, stride=2), :] = jnp.where(mask, p, 0.0)
    rows[pl.ds(1, ROWS, stride=2), :] = jnp.where(mask, 0.0, p)
    return jnp.concatenate(split(rows[...]), 1)


def quadrants(total):
    n = total.shape[0] // 2
    return total[:n, :n] + total[:n, n:] + total[n:, :n] + total[n:, n:]


def add_rows(total, a, b):
    total[...] += lax.dot_general(
        a, b, (((0,), (0,)), ((), ())), preferred_element_type=F32
    )


def right_step(c, p_ref, g_ref, e_ref, sides, q_total, rows, mask):
    for j in range(STEP):
        sides[c * STEP + j] = interleave(p_ref[c * STEP + j], rows.at[j], mask)
    blocks = pl.ds(c * STEP, STEP)
    depth = STEP * 2 * ROWS
    x = jnp.concatenate(
        [g_ref[blocks].reshape(depth, 128), e_ref[blocks].reshape(depth, 128)], 1
    )
    add_rows(q_total, sides[blocks].reshape(depth, 256), x)


RIGHT_SCRATCH = [pltpu.VMEM((256, 256), F32), pltpu.VMEM((STEP, 2 * ROWS, 128), F32)]


def right_kernel(p_ref, g_ref, e_ref, q_ref, gram_ref, sides, gram_total, q_total, rows):
    q_total[...] = jnp.zeros_like(q_total)
    gram_total[...] = jnp.zeros_like(gram_total)
    mask = first_projection((ROWS, 2 * R))
    for c in range(BLOCKS // STEP):
        right_step(c, p_ref, g_ref, e_ref, sides, q_total, rows, mask)
        for j in range(STEP):
            plain = jnp.concatenate(split(p_ref[c * STEP + j]), 1)
            add_rows(gram_total, plain, plain)

    q_ref[...] = quadrants(q_total[...])
    gram_ref[...] = quadrants(gram_total[...])


def right_half(p, g, e):
    square = jax.ShapeDtypeStruct((128, 128), F32)
    return pl.pallas_call(
        right_kernel,
        in_specs=[VMEM] * 3,
        out_specs=[VMEM] * 3,
        out_shape=[square, square, pltpu.VMEM(HALF_S, BF16)],
        scratch_shapes=[pltpu.VMEM((256, 256), F32), *RIGHT_SCRATCH],
        compiler_params=pltpu.CompilerParams(vmem_limit_bytes=LIMIT),
        cost_estimate=pl.CostEstimate(
            flops=3 * 8192 * 256 * 256, bytes_accessed=6 * 2**20, transcendentals=0
        ),
        name="right_half",
    )(in_vmem(p), in_vmem(g), in_vmem(e))


def inverse_of_factor(gram):
    mask = first_projection((R, 2 * R))
    lane = lax.broadcasted_iota(jnp.int32, (R, 2 * R), 1)
    row = lax.broadcasted_iota(jnp.int32, (R, 2 * R), 0)
    rest = jnp.where(mask, gram[:R], gram[R:])
    inverse = jnp.where(lane % R == row, 1.0, 0.0).astype(F32)
    pivots = jnp.ones((R, 2 * R), F32)
    for start in range(0, R, PANEL):
        panel = [
            jnp.where(mask, rest[:, j : j + 1], rest[:, R + j : R + j + 1])
            for j in range(start, start + PANEL)
        ]
        for i in range(0, PANEL, 2):
            j = start + i
            first, second = panel[i], panel[i + 1]
            a, b, c = first[j : j + 1], first[j + 1 : j + 2], second[j + 1 : j + 2]
            a_inverse = 1.0 / a
            ratio = b * a_inverse
            rest_c = c - b * ratio
            pivots = jnp.where(row == j, a, pivots)
            pivots = jnp.where(row == j + 1, rest_c, pivots)
            one = jnp.where(row > j, first * a_inverse, 0.0)
            two = (second - one * b) * (1.0 / rest_c)
            two = jnp.where(row > j + 1, two, 0.0)

            def eliminate(matrix):
                upper = matrix[j : j + 1]
                lower = matrix[j + 1 : j + 2] - ratio * upper
                return matrix - one * upper - two * lower

            for m in range(i + 2, PANEL):
                panel[m] = eliminate(panel[m])
            inverse = eliminate(inverse)
            rest = eliminate(rest)
    return inverse * lax.rsqrt(pivots)


def by_core(first, second):
    low = lax.axis_index("core") == 0
    return jnp.where(low, first, second), jnp.where(low, second, first)


def other_kernel(p_ref, g_ref, e_ref, q_in, keep_ref, send_ref, sides, q_total, rows):
    q_total[...] = jnp.zeros_like(q_total)
    mask = first_projection((ROWS, 2 * R))
    for c in range(BLOCKS // STEP):
        right_step(c, p_ref, g_ref, e_ref, sides, q_total, rows, mask)
    q = quadrants(q_total[...]) + q_in[...]
    keep_ref[...], send_ref[...] = by_core(q[:R], q[R:])


def other_half(p, g, e, q):
    part = jax.ShapeDtypeStruct((R, 128), F32)
    return pl.pallas_call(
        other_kernel,
        in_specs=[VMEM] * 4,
        out_specs=[VMEM] * 3,
        out_shape=[part, part, pltpu.VMEM(HALF_S, BF16)],
        scratch_shapes=RIGHT_SCRATCH,
        compiler_params=pltpu.CompilerParams(vmem_limit_bytes=LIMIT),
        cost_estimate=pl.CostEstimate(
            flops=2 * 8192 * 256 * 256, bytes_accessed=6 * 2**20, transcendentals=0
        ),
        name="other_half",
    )(in_vmem(p), in_vmem(g), in_vmem(e), q)


def solve_kernel(gram_in, gram_other, p_mine, p_other, after, inverse_ref, factors_ref):
    solved = inverse_of_factor(gram_in[...] + gram_other[...])
    side = first_projection((R, 2 * R))
    inverse = jnp.concatenate([jnp.where(side, solved, 0.0), jnp.where(side, 0.0, solved)], 0)
    inverse_ref[...] = inverse
    core = lax.axis_index("core")
    block = lax.axis_index("z") * 2 + core
    p = jnp.where(lax.axis_index("x_hi") == core, p_mine[block], p_other[block])
    factors_ref[...] = split_dot(inverse, p, 1, 1).astype(BF16)


def solve(gram, gram_other, p_mine, p_other, after):
    return pl.pallas_call(
        solve_kernel,
        in_specs=[VMEM] * 5,
        out_specs=[VMEM] * 2,
        out_shape=[
            jax.ShapeDtypeStruct((128, 128), F32),
            jax.ShapeDtypeStruct((128, ROWS), BF16),
        ],
        compiler_params=pltpu.CompilerParams(vmem_limit_bytes=LIMIT),
        cost_estimate=pl.CostEstimate(
            flops=2**30, bytes_accessed=2**20, transcendentals=0
        ),
        name="solve",
    )(gram, gram_other, in_vmem(p_mine), in_vmem(p_other), after)


def mean_kernel(pieces, inverse_ref, q_ref, norm_ref):
    total = pieces[0]
    for i in range(1, pieces.shape[0]):
        total = total + pieces[i]
    upper, _ = by_core(inverse_ref[:R], inverse_ref[R:])
    q_mean = split_dot(upper, jnp.concatenate([total, total], 0), 1, 0) * (1.0 / REPLICAS)
    q_ref[...] = q_mean
    norm_ref[...] = jnp.full(norm_ref.shape, jnp.sum(q_mean * q_mean), F32)


def mean(pieces, inverse):
    return pl.pallas_call(
        mean_kernel,
        in_specs=[VMEM] * 2,
        out_specs=[VMEM] * 2,
        out_shape=[
            jax.ShapeDtypeStruct((R, 128), F32),
            jax.ShapeDtypeStruct((16, 128), F32),
        ],
        compiler_params=pltpu.CompilerParams(vmem_limit_bytes=LIMIT),
        name="mean",
    )(pieces, inverse)


def error_kernel(inverse_ref, q_mine, q_other, norm_parts, *rest):
    halves, (out_hbm, q_hbm, q_staged, q_sent, weights, staged, sent) = (rest[:3], rest[3:6]), rest[6:]
    core = lax.axis_index("core")
    q_mean = jnp.concatenate(by_core(q_mine[...], q_other[...]), 0)
    norm_square = jnp.sum(norm_parts[...], 0, keepdims=True)
    clip_limit = 0.5 * (2 * KVW * R) ** 0.5
    q_staged[...] = q_mean * jnp.minimum(1.0, clip_limit / jnp.sqrt(norm_square))
    copies = [pltpu.make_async_copy(q_staged, q_hbm, q_sent)]
    copies[0].start()
    high, low = split(split_dot(inverse_ref[...], q_mean, 0, 0))
    line = jnp.concatenate([high, low], 1)
    weights[...] = jnp.concatenate([line, line], 0)
    for h, (sides, g_ref, e_ref) in enumerate(halves):
        for block in range(BLOCKS):
            approx = jnp.dot(sides[block], weights[...], preferred_element_type=F32)
            compensated = g_ref[block].astype(F32) + e_ref[block].astype(F32)
            left = compensated - (approx[:, :128] + approx[:, 128:])
            staged[h, block] = left.astype(BF16)
            if (block + 1) % SEND == 0:
                blocks = pl.ds(block + 1 - SEND, SEND)
                place = core if h == 0 else 1 - core
                copies.append(
                    pltpu.make_async_copy(
                        staged.at[h, blocks], out_hbm.at[place, blocks], sent.at[h, block // SEND]
                    )
                )
                copies[-1].start()
    for copy in copies:
        copy.wait()


def errors_out(inverse, q_mine, q_other, norm_parts, mine, other):
    return pl.pallas_call(
        error_kernel,
        in_specs=[VMEM] * 10,
        out_specs=[ANY, ANY],
        out_shape=[
            jax.ShapeDtypeStruct((2, BLOCKS, 2 * ROWS, 128), BF16),
            jax.ShapeDtypeStruct((128, 128), F32),
        ],
        scratch_shapes=[
            pltpu.VMEM((128, 128), F32),
            pltpu.SemaphoreType.DMA,
            pltpu.VMEM((256, 256), BF16),
            pltpu.VMEM((2, *HALF_X), BF16),
            pltpu.SemaphoreType.DMA((2, BLOCKS // SEND)),
        ],
        compiler_params=pltpu.CompilerParams(vmem_limit_bytes=LIMIT),
        cost_estimate=pl.CostEstimate(
            flops=2 * 16384 * 256 * 256, bytes_accessed=16 * 2**20, transcendentals=0
        ),
        name="new_errors",
    )(inverse, q_mine, q_other, norm_parts, *[in_vmem(a) for a in (*mine, *other)])


def sum_kernel(pieces, out_ref):
    total = pieces[0]
    for i in range(1, pieces.shape[0]):
        total = total + pieces[i]
    if len(out_ref.shape) == 2:
        out_ref[...] = total
    else:
        for i in range(out_ref.shape[0]):
            out_ref[i] = total


def sum_pieces(pieces, copies=None):
    shape = pieces.shape[1:] if copies is None else (copies, *pieces.shape[1:])
    return pl.pallas_call(
        sum_kernel,
        in_specs=[VMEM],
        out_specs=VMEM,
        out_shape=jax.ShapeDtypeStruct(shape, F32),
        compiler_params=pltpu.CompilerParams(vmem_limit_bytes=LIMIT),
        name="sum_pieces",
    )(pieces)


def place_kernel(own, *rest):
    *others, out_ref = rest
    core, z = lax.axis_index("core"), lax.axis_index("z")
    pair = (z + core) % 2
    place = jnp.where(core == 0, lax.axis_index("x_hi") * 2 + lax.axis_index("x_lo"), lax.axis_index("y"))
    out_ref[pair * 4 + place] = own[...]
    for (flip, shift), block in zip(WAYS, others):
        out_ref[(pair + flip) % 2 * 4 + (place + 4 - shift) % 4] = block[...]


def gather_near(block):
    others = [lax.ppermute(block, AXES, way_pairs(*way)) for way in WAYS]
    return pl.pallas_call(
        place_kernel,
        in_specs=[VMEM] * 8,
        out_specs=VMEM,
        out_shape=pltpu.VMEM((8, *block.shape), F32),
        compiler_params=pltpu.CompilerParams(vmem_limit_bytes=LIMIT),
        name="gather_near",
    )(block, *others)


def add_kernel(a_ref, b_ref, after, out_ref):
    total = a_ref[...] + b_ref[...]
    for i in range(out_ref.shape[0]):
        out_ref[i] = total


def add_for_each(a, b, copies, after):
    return pl.pallas_call(
        add_kernel,
        in_specs=[VMEM] * 3,
        out_specs=VMEM,
        out_shape=jax.ShapeDtypeStruct((copies, *a.shape), F32),
        compiler_params=pltpu.CompilerParams(vmem_limit_bytes=LIMIT),
        name="add_for_each",
    )(a, b, after)


def swap(value, axis="core"):
    return lax.ppermute(value, axis, [(0, 1), (1, 0)])


def per_device(grads, errors, q_prev):
    g = grads.reshape(2, BLOCKS, 2 * ROWS, 128)
    e = errors.reshape(2, BLOCKS, 2 * ROWS, 128)
    qt = q_prev.transpose(0, 2, 1).reshape(2 * R, 128)

    part_other, g_other, e_other = left_half(False, g, e, qt)
    sent = swap(part_other)
    part, g_mine, e_mine = left_half(True, g, e, qt)
    part = exchange((part + sent).reshape(8, 512, 128), NEAR)
    part = sum_pieces(part).reshape(16, 32, 128)
    part = sum_pieces(exchange(part, FAR), 16)
    part = exchange(part, FAR).reshape(512, 128)
    p_mine = gather_near(part).reshape(HALF_P)
    p_other = swap(p_mine)

    q_part, gram, sides_mine = right_half(p_mine, g_mine, e_mine)
    gram_other = swap(gram)
    q_keep, q_send, sides_other = other_half(p_other, g_other, e_other, q_part)

    q_chip = q_keep + swap(q_send)
    q_sent = swap(q_chip, "x_hi")
    inverse, p_factors = solve(gram, gram_other, p_mine, p_other, q_chip)
    q_chips = add_for_each(q_chip, q_sent, 8, inverse)
    q_chips = lax.all_to_all(q_chips, "z", 0, 0, tiled=True)
    q_mine, norm_part = mean(q_chips, inverse)
    q_other = swap(q_mine)
    norm_parts = lax.all_to_all(norm_part[:, None], BLOCK, 0, 0, tiled=True)

    new_errors, q_factors = errors_out(
        inverse,
        q_mine,
        q_other,
        norm_parts.reshape(16, 128),
        (sides_mine, g_mine, e_mine),
        (sides_other, g_other, e_other),
    )
    return (
        new_errors.reshape(1, D, 2, 128),
        p_factors.reshape(2, R, ROWS).transpose(0, 2, 1),
        q_factors.reshape(2, R, 128).transpose(0, 2, 1),
    )


def solution(mesh):
    named = Mesh(mesh.devices.reshape(2, 8, 2, 4, 2), AXES)
    in_specs = (
        P(REPLICA, None, None, TENSOR),
        P(REPLICA, None, None, TENSOR),
        P(None, TENSOR, None),
    )
    out_specs = (P(REPLICA, None, None, TENSOR), P(None, REPLICA, None), P(None, TENSOR, None))
    return jax.shard_map(
        per_device, mesh=named, in_specs=in_specs, out_specs=out_specs, check_vma=False
    )
```

profile of v0, /device:TPU:1, one launch (start us, length us, event | category | flops | bytes accessed | tf_op | source)
XLA Modules:
  0.0 130.1 jit_solution(10249869449160852401)
XLA Ops:
  0.6 3.6 %left_half.3 = (f32[16,256,128]{2,1,0:T(8,128)S(1)}, bf16[16,512,128]{2,1,0:T(8,128)(2,1)S(1)}, bf16[16,512,128]{2,1,0:T(8,128)(2,1)S(1)}) custom-call(bf16[2,16,512,128]{3,2,1,0:T(8,128)(2,1)} %bitcast.34, bf16[2,16,512,128]{3,2,1,0:T(8,128)(2,1)} %bitcast.36, f32[128,128]{1,0:T(8,128)} %bitcast.39), custom_call_target="tpu_custom_call" | custom-call | flops 1073741824 | bytes 8388608 | tf_op jit(solution)/shard_map/left_half/pallas_call | solution.py:148
  4.2 3.3 %collective-permute-start = (f32[16,256,128]{2,1,0:T(8,128)S(1)}, f32[16,256,128]{2,1,0:T(8,128)S(1)}, u32[]{:S(2)}, u32[]{:S(2)}) collective-permute-start(f32[16,256,128]{2,1,0:T(8,128)S(1)} %get-tuple-element.22), channel_id=1, source_target_pairs={{0,8},{8,0},{1,9},{9,1},{2,10},{10,2},{3,11},{11,3},{4,12},{12,4},... | collective-permute-start | bytes 6291464 | tf_op jit(solution)/shard_map/ppermute | solution.py:470
  7.5 3.6 %left_half.2 = (f32[16,256,128]{2,1,0:T(8,128)S(1)}, bf16[16,512,128]{2,1,0:T(8,128)(2,1)S(1)}, bf16[16,512,128]{2,1,0:T(8,128)(2,1)S(1)}) custom-call(bf16[2,16,512,128]{3,2,1,0:T(8,128)(2,1)} %bitcast.35, bf16[2,16,512,128]{3,2,1,0:T(8,128)(2,1)} %bitcast.37, f32[128,128]{1,0:T(8,128)} %bitcast.40), custom_call_target="tpu_custom_call" | custom-call | flops 1073741824 | bytes 8388608 | tf_op jit(solution)/shard_map/left_half/pallas_call | solution.py:148
  11.1 0.2 collective-permute-done
  11.3 0.3 add.6
  11.6 22.6 %all_to_all.25.pieces = f32[8,512,128]{2,1,0:T(8,128)S(1)} all-to-all(f32[8,512,128]{2,1,0:T(8,128)S(1)} %bitcast.38), channel_id=1, replica_groups={{0,1,128,129,16,17,144,145},{32,33,160,161,48,49,176,177},{64,65,192,19..., dimensions={0} | all-to-all | bytes 4194304 | tf_op jit(solution)/shard_map/all_to_all | solution.py:68
  34.2 0.1 sum_pieces.2
  34.3 19.7 %all_to_all.26.pieces = f32[16,32,128]{2,1,0:T(8,128)S(1)} all-to-all(f32[16,32,128]{2,1,0:T(8,128)S(1)} %bitcast.31), channel_id=1, replica_groups={{0,2,4,6,32,34,36,38,64,66,68,70,96,98,100,102},{16,18,20,22,48,50,52,5..., dimensions={0} | all-to-all | bytes 524288 | tf_op jit(solution)/shard_map/all_to_all | solution.py:68
  54.1 16.2 %all_to_all.27 = f32[16,32,128]{2,1,0:T(8,128)S(1)} all-to-all(f32[16,32,128]{2,1,0:T(8,128)S(1)} %sum_pieces.3), channel_id=1, replica_groups={{0,2,4,6,32,34,36,38,64,66,68,70,96,98,100,102},{16,18,20,22,48,50,52,5..., dimensions={0} | all-to-all | bytes 524288 | tf_op jit(solution)/shard_map/all_to_all | solution.py:68
  70.2 0.0 collective-permute-start.7
  70.2 4.1 %collective-permute-start.6 = (f32[512,128]{1,0:T(8,128)S(1)}, f32[512,128]{1,0:T(8,128)S(1)}, u32[]{:S(2)}, u32[]{:S(2)}) collective-permute-start(f32[512,128]{1,0:T(8,128)S(1)} %bitcast.24), channel_id=1, source_target_pairs={{0,145},{1,16},{128,17},{129,144},{16,129},{17,0},{144,1},{145,128... | collective-permute-start | bytes 786440 | tf_op jit(solution)/shard_map/ppermute | solution.py:441
  74.3 0.0 collective-permute-start.5
  74.3 1.2 collective-permute-start.4
  75.5 1.9 %collective-permute-start.3 = (f32[512,128]{1,0:T(8,128)S(1)}, f32[512,128]{1,0:T(8,128)S(1)}, u32[]{:S(2)}, u32[]{:S(2)}) collective-permute-start(f32[512,128]{1,0:T(8,128)S(1)} %bitcast.27), channel_id=1, source_target_pairs={{0,129},{1,0},{128,1},{129,128},{16,145},{17,16},{144,17},{145,144... | collective-permute-start | bytes 786440 | tf_op jit(solution)/shard_map/ppermute | solution.py:441
  77.4 1.8 %collective-permute-done.7.rest_6_ = f32[512,128]{1,0:T(8,128)S(1)} collective-permute-done((f32[512,128]{1,0:T(8,128)S(1)}, f32[512,128]{1,0:T(8,128)S(1)}, u32[]{:S(2)}, u32[]{:S(2)}) %collective-permute-start.7) | collective-permute-done | bytes 262176 | tf_op jit(solution)/shard_map/ppermute | solution.py:441
  79.1 0.0 collective-permute-start.2
  79.1 2.2 %collective-permute-done.6.rest_5_ = f32[512,128]{1,0:T(8,128)S(1)} collective-permute-done((f32[512,128]{1,0:T(8,128)S(1)}, f32[512,128]{1,0:T(8,128)S(1)}, u32[]{:S(2)}, u32[]{:S(2)}) %collective-permute-start.6) | collective-permute-done | bytes 262176 | tf_op jit(solution)/shard_map/ppermute | solution.py:441
  81.4 0.0 collective-permute-start.1
  81.4 3.4 %collective-permute-done.5.rest_4_ = f32[512,128]{1,0:T(8,128)S(1)} collective-permute-done((f32[512,128]{1,0:T(8,128)S(1)}, f32[512,128]{1,0:T(8,128)S(1)}, u32[]{:S(2)}, u32[]{:S(2)}) %collective-permute-start.5) | collective-permute-done | bytes 262176 | tf_op jit(solution)/shard_map/ppermute | solution.py:441
  84.8 0.0 collective-permute-done.4.rest_3_
  84.8 2.2 %collective-permute-done.3.rest_2_ = f32[512,128]{1,0:T(8,128)S(1)} collective-permute-done((f32[512,128]{1,0:T(8,128)S(1)}, f32[512,128]{1,0:T(8,128)S(1)}, u32[]{:S(2)}, u32[]{:S(2)}) %collective-permute-start.3) | collective-permute-done | bytes 262176 | tf_op jit(solution)/shard_map/ppermute | solution.py:441
  87.0 0.8 collective-permute-done.2.rest_1_
  87.8 0.3 collective-permute-done.1.rest_0_
  88.1 0.2 gather_near.1
  88.3 0.9 collective-permute-start.9
  89.1 2.2 %right_half.1 = (f32[128,128]{1,0:T(8,128)S(1)}, f32[128,128]{1,0:T(8,128)S(1)}, bf16[16,512,256]{2,1,0:T(8,128)(2,1)S(1)}) custom-call(f32[16,256,128]{2,1,0:T(8,128)S(1)} %bitcast.21, bf16[16,512,128]{2,1,0:T(8,128)(2,1)S(1)} %get-tuple-element.23.g_ref.rest_1_, bf16[16,512,128]{2,1,0:T(8,128)(2,1)S(1)} %get-tuple-element.24.e_ref.rest_2_), custom_call_target="tpu_custom_call" | custom-call | flops 1610612736 | bytes 6291456 | tf_op jit(solution)/shard_map/right_half/pallas_call | solution.py:219
  91.4 0.3 collective-permute-start.8
  91.7 1.3 collective-permute-done.9.p_ref.p_other
  92.9 1.8 %other_half.1 = (f32[64,128]{1,0:T(8,128)S(1)}, f32[64,128]{1,0:T(8,128)S(1)}, bf16[16,512,256]{2,1,0:T(8,128)(2,1)S(1)}) custom-call(f32[16,256,128]{2,1,0:T(8,128)S(1)} %collective-permute-done.9.p_ref.p_other, bf16[16,512,128]{2,1,0:T(8,128)(2,1)S(1)} %get-tuple-element.26.g_ref.rest_4_, bf16[16,512,128]{2,1,0:T(8,128)(2,1)S(1)} %get-tuple-element.27.e_ref.rest_5_, ...), custom_call_target="tpu_custom_call" | custom-call | flops 1073741824 | bytes 6291456 | tf_op jit(solution)/shard_map/other_half/pallas_call | solution.py:286
  94.7 0.5 collective-permute-start.10
  95.2 0.9 collective-permute-done.10
  96.0 0.8 collective-permute-start.11
  96.9 0.0 collective-permute-done.8.gram_other
  96.9 2.5 %solve.1 = (f32[128,128]{1,0:T(8,128)S(1)}, bf16[128,256]{1,0:T(8,128)(2,1)}) custom-call(f32[128,128]{1,0:T(8,128)S(1)} %get-tuple-element.25.gram_in, f32[128,128]{1,0:T(8,128)S(1)} %collective-permute-done.8.gram_other, f32[16,256,128]{2,1,0:T(8,128)S(1)} %bitcast.22, f32[16,256,128]{2,1,0:T(8,128)S(1)} %collective-permute-done.9.p_ref.p_other, ...), custom_call_target="tpu_custom_call" | custom-call | flops 1073741824 | bytes 1048576 | tf_op jit(solution)/shard_map/solve/pallas_call | solution.py:312
  99.4 0.9 collective-permute-done.11.b_ref
  100.3 12.8 %all_to_all.28.pieces = f32[8,64,128]{2,1,0:T(8,128)S(1)} all-to-all(f32[8,64,128]{2,1,0:T(8,128)S(1)} %add_for_each.1), channel_id=1, replica_groups=mesh['x_hi'=2,'z'=8,'core'=2,'y'=4,'x_lo'=2] {'z'}, dimensions={0} | all-to-all | bytes 524288 | tf_op jit(solution)/shard_map/all_to_all | solution.py:496
  113.2 0.3 mean.1
  113.5 3.4 %collective-permute-start.12 = (f32[64,128]{1,0:T(8,128)S(1)}, f32[64,128]{1,0:T(8,128)S(1)}, u32[]{:S(2)}, u32[]{:S(2)}) collective-permute-start(f32[64,128]{1,0:T(8,128)S(1)} %get-tuple-element.32.q_mine), channel_id=1, source_target_pairs={{0,8},{8,0},{1,9},{9,1},{2,10},{10,2},{3,11},{11,3},{4,12},{12,4},... | collective-permute-start | bytes 98312 | tf_op jit(solution)/shard_map/ppermute | solution.py:470
  116.8 9.6 %all_to_all.29 = f32[16,1,128]{2,1,0:T(1,128)S(1)} all-to-all(f32[16,1,128]{2,1,0:T(1,128)S(1)} %bitcast.33), channel_id=1, replica_groups=mesh['x_hi'=2,'z'=8,'core'=2,'y'=4,'x_lo'=2] {'core','y','x_lo'}, dimensions={0} | all-to-all | bytes 16384 | tf_op jit(solution)/shard_map/all_to_all | solution.py:499
  126.5 0.0 collective-permute-done.12.q_other
  126.5 3.5 %new_errors.1 = (bf16[2,16,512,128]{3,2,1,0:T(8,128)(2,1)}, f32[128,128]{1,0:T(8,128)}) custom-call(f32[128,128]{1,0:T(8,128)S(1)} %get-tuple-element.31.after.inverse_ref, f32[64,128]{1,0:T(8,128)S(1)} %get-tuple-element.32.q_mine, f32[64,128]{1,0:T(8,128)S(1)} %collective-permute-done.12.q_other, f32[16,128]{1,0:T(8,128)S(1)} %bitcast.32, ...), custom_call_target="tpu_custom_call" | custom-call | flops 2147483648 | bytes 16777216 | tf_op jit(solution)/shard_map/new_errors/pallas_call | solution.py:384
  (3 shorter events, 0.1 us)
Async XLA Ops:
  4.2 7.1 %collective-permute-start = (f32[16,256,128]{2,1,0:T(8,128)S(1)}, f32[16,256,128]{2,1,0:T(8,128)S(1)}, u32[]{:S(2)}, u32[]{:S(2)}) collective-permute-start(f32[16,256,128]{2,1,0:T(8,128)S(1)} %get-tuple-element.22), channel_id=1, source_target_pairs={{0,8},{8,0},{1,9},{9,1},{2,10},{10,2},{3,11},{11,3},{4,12},{12,4},... | collective-permute-start | bytes 6291464 | tf_op jit(solution)/shard_map/ppermute | solution.py:470
  70.2 8.9 %collective-permute-start.7 = (f32[512,128]{1,0:T(8,128)S(1)}, f32[512,128]{1,0:T(8,128)S(1)}, u32[]{:S(2)}, u32[]{:S(2)}) collective-permute-start(f32[512,128]{1,0:T(8,128)S(1)} %bitcast.23), channel_id=1, source_target_pairs={{0,144},{1,145},{128,16},{129,17},{16,128},{17,129},{144,0},{145,1... | collective-permute-start | bytes 786440 | tf_op jit(solution)/shard_map/ppermute | solution.py:441
  70.2 11.1 %collective-permute-start.6 = (f32[512,128]{1,0:T(8,128)S(1)}, f32[512,128]{1,0:T(8,128)S(1)}, u32[]{:S(2)}, u32[]{:S(2)}) collective-permute-start(f32[512,128]{1,0:T(8,128)S(1)} %bitcast.24), channel_id=1, source_target_pairs={{0,145},{1,16},{128,17},{129,144},{16,129},{17,0},{144,1},{145,128... | collective-permute-start | bytes 786440 | tf_op jit(solution)/shard_map/ppermute | solution.py:441
  74.3 10.5 %collective-permute-start.5 = (f32[512,128]{1,0:T(8,128)S(1)}, f32[512,128]{1,0:T(8,128)S(1)}, u32[]{:S(2)}, u32[]{:S(2)}) collective-permute-start(f32[512,128]{1,0:T(8,128)S(1)} %bitcast.25), channel_id=1, source_target_pairs={{0,17},{1,144},{128,145},{129,16},{16,1},{17,128},{144,129},{145,0... | collective-permute-start | bytes 786440 | tf_op jit(solution)/shard_map/ppermute | solution.py:441
  74.3 10.5 %collective-permute-start.4 = (f32[512,128]{1,0:T(8,128)S(1)}, f32[512,128]{1,0:T(8,128)S(1)}, u32[]{:S(2)}, u32[]{:S(2)}) collective-permute-start(f32[512,128]{1,0:T(8,128)S(1)} %bitcast.26), channel_id=1, source_target_pairs={{0,128},{1,129},{128,0},{129,1},{16,144},{17,145},{144,16},{145,17... | collective-permute-start | bytes 786440 | tf_op jit(solution)/shard_map/ppermute | solution.py:441
  75.5 11.5 %collective-permute-start.3 = (f32[512,128]{1,0:T(8,128)S(1)}, f32[512,128]{1,0:T(8,128)S(1)}, u32[]{:S(2)}, u32[]{:S(2)}) collective-permute-start(f32[512,128]{1,0:T(8,128)S(1)} %bitcast.27), channel_id=1, source_target_pairs={{0,129},{1,0},{128,1},{129,128},{16,145},{17,16},{144,17},{145,144... | collective-permute-start | bytes 786440 | tf_op jit(solution)/shard_map/ppermute | solution.py:441
  79.1 8.6 %collective-permute-start.2 = (f32[512,128]{1,0:T(8,128)S(1)}, f32[512,128]{1,0:T(8,128)S(1)}, u32[]{:S(2)}, u32[]{:S(2)}) collective-permute-start(f32[512,128]{1,0:T(8,128)S(1)} %bitcast.28), channel_id=1, source_target_pairs={{0,1},{1,128},{128,129},{129,0},{16,17},{17,144},{144,145},{145,16... | collective-permute-start | bytes 786440 | tf_op jit(solution)/shard_map/ppermute | solution.py:441
  81.4 6.7 %collective-permute-start.1 = (f32[512,128]{1,0:T(8,128)S(1)}, f32[512,128]{1,0:T(8,128)S(1)}, u32[]{:S(2)}, u32[]{:S(2)}) collective-permute-start(f32[512,128]{1,0:T(8,128)S(1)} %bitcast.29), channel_id=1, source_target_pairs={{0,16},{1,17},{128,144},{129,145},{16,0},{17,1},{144,128},{145,129... | collective-permute-start | bytes 786440 | tf_op jit(solution)/shard_map/ppermute | solution.py:441
  88.3 4.7 %collective-permute-start.9 = (f32[16,256,128]{2,1,0:T(8,128)S(1)}, f32[16,256,128]{2,1,0:T(8,128)S(1)}, u32[]{:S(2)}, u32[]{:S(2)}) collective-permute-start(f32[16,256,128]{2,1,0:T(8,128)S(1)} %bitcast.20), channel_id=1, source_target_pairs={{0,8},{8,0},{1,9},{9,1},{2,10},{10,2},{3,11},{11,3},{4,12},{12,4},... | collective-permute-start | bytes 6291464 | tf_op jit(solution)/shard_map/ppermute | solution.py:470
  91.4 5.5 %collective-permute-start.8 = (f32[128,128]{1,0:T(8,128)S(1)}, f32[128,128]{1,0:T(8,128)S(1)}, u32[]{:S(2)}, u32[]{:S(2)}) collective-permute-start(f32[128,128]{1,0:T(8,128)S(1)} %get-tuple-element.25.gram_in), channel_id=1, source_target_pairs={{0,8},{8,0},{1,9},{9,1},{2,10},{10,2},{3,11},{11,3},{4,12},{12,4},... | collective-permute-start | bytes 196616 | tf_op jit(solution)/shard_map/ppermute | solution.py:470
  94.7 1.3 %collective-permute-start.10 = (f32[64,128]{1,0:T(8,128)S(1)}, f32[64,128]{1,0:T(8,128)S(1)}, u32[]{:S(2)}, u32[]{:S(2)}) collective-permute-start(f32[64,128]{1,0:T(8,128)S(1)} %get-tuple-element.30), channel_id=1, source_target_pairs={{0,8},{8,0},{1,9},{9,1},{2,10},{10,2},{3,11},{11,3},{4,12},{12,4},... | collective-permute-start | bytes 98312 | tf_op jit(solution)/shard_map/ppermute | solution.py:470
  96.0 4.3 %collective-permute-start.11 = (f32[64,128]{1,0:T(8,128)S(1)}, f32[64,128]{1,0:T(8,128)S(1)}, u32[]{:S(2)}, u32[]{:S(2)}) collective-permute-start(f32[64,128]{1,0:T(8,128)S(1)} %add.7.after.a_ref), channel_id=1, source_target_pairs={{0,128},{128,0},{1,129},{129,1},{2,130},{130,2},{3,131},{131,3},{4... | collective-permute-start | bytes 98312 | tf_op jit(solution)/shard_map/ppermute | solution.py:470
  113.5 13.0 %collective-permute-start.12 = (f32[64,128]{1,0:T(8,128)S(1)}, f32[64,128]{1,0:T(8,128)S(1)}, u32[]{:S(2)}, u32[]{:S(2)}) collective-permute-start(f32[64,128]{1,0:T(8,128)S(1)} %get-tuple-element.32.q_mine), channel_id=1, source_target_pairs={{0,8},{8,0},{1,9},{9,1},{2,10},{10,2},{3,11},{11,3},{4,12},{12,4},... | collective-permute-start | bytes 98312 | tf_op jit(solution)/shard_map/ppermute | solution.py:470
where the time goes:
time: 130 us
  blocking collectives  81 us (62%)
  Pallas kernels  17.8 us (14%)
  starting transfers between devices  16.3 us (13%)
  waiting for transfers between devices  14 us (11%)
    all_to_all x3, blocking collectives, exchange(): lax.all_to_all(pieces, AXES, 0, 0, axis_index_groups=groups, tiled=True)  58.5 us
    all_to_all x1, blocking collectives, per_device(): q_chips = lax.all_to_all(q_chips, 'z', 0, 0, tiled=True)  12.8 us
    ppermute x7, waiting for transfers between devices, gather_near(): others = [lax.ppermute(block, AXES, way_pairs(*way)) for way in WAYS]  10.7 us
    all_to_all x1, blocking collectives, per_device(): norm_parts = lax.all_to_all(norm_part[:, None], BLOCK, 0, 0, tiled=True)  9.62 us
    ppermute x6, starting transfers between devices, swap(): return lax.ppermute(value, axis, [(0, 1), (1, 0)])  9.15 us
    ppermute x7, starting transfers between devices, gather_near(): others = [lax.ppermute(block, AXES, way_pairs(*way)) for way in WAYS]  7.16 us
    pallas_call x2, Pallas kernels, left_half(): pl.pallas_call(functools.partial(left_kernel, mine), in_specs=[ANY, ANY,...  7.11 us
    pallas_call x1, Pallas kernels, errors_out(): pl.pallas_call(error_kernel, in_specs=[VMEM] * 10, out_specs=[ANY, ANY],...  3.51 us
  transfers between devices with their start and end apart: 13, of which 10 were waited for; matrix products, arithmetic and copies ran while one was open for 0% of the time, Pallas kernels for 8%

commit v1 on v0

--- a/solution.py
+++ b/solution.py
@@ -449,6 +449,45 @@
     )(block, *others)
 
 
+def pieces_kernel(a_ref, b_ref, own, *others):
+    core, z = lax.axis_index("core"), lax.axis_index("z")
+    pair = (z + core) % 2
+    place = jnp.where(core == 0, lax.axis_index("x_hi") * 2 + lax.axis_index("x_lo"), lax.axis_index("y"))
+    at = pair * 4 + place
+    own[...] = a_ref[at] + b_ref[at]
+    for (flip, shift), out_ref in zip(WAYS, others):
+        there = (pair + flip) % 2 * 4 + (place + shift) % 4
+        out_ref[...] = a_ref[there] + b_ref[there]
+
+
+def total_kernel(*refs):
+    total = refs[0][...]
+    for ref in refs[1:-1]:
+        total = total + ref[...]
+    refs[-1][...] = total
+
+
+def sum_near(a, b):
+    piece = pltpu.VMEM(a.shape[1:], F32)
+    own, *others = pl.pallas_call(
+        pieces_kernel,
+        in_specs=[VMEM] * 2,
+        out_specs=[VMEM] * 8,
+        out_shape=[piece] * 8,
+        compiler_params=pltpu.CompilerParams(vmem_limit_bytes=LIMIT),
+        name="near_pieces",
+    )(a, b)
+    others = [lax.ppermute(o, AXES, way_pairs(*way)) for o, way in zip(others, WAYS)]
+    return pl.pallas_call(
+        total_kernel,
+        in_specs=[VMEM] * 8,
+        out_specs=VMEM,
+        out_shape=jax.ShapeDtypeStruct(a.shape[1:], F32),
+        compiler_params=pltpu.CompilerParams(vmem_limit_bytes=LIMIT),
+        name="sum_near",
+    )(own, *others)
+
+
 def add_kernel(a_ref, b_ref, after, out_ref):
     total = a_ref[...] + b_ref[...]
     for i in range(out_ref.shape[0]):
@@ -478,8 +517,7 @@
     part_other, g_other, e_other = left_half(False, g, e, qt)
     sent = swap(part_other)
     part, g_mine, e_mine = left_half(True, g, e, qt)
-    part = exchange((part + sent).reshape(8, 512, 128), NEAR)
-    part = sum_pieces(part).reshape(16, 32, 128)
+    part = sum_near(part.reshape(8, 512, 128), sent.reshape(8, 512, 128)).reshape(16, 32, 128)
     part = sum_pieces(exchange(part, FAR), 16)
     part = exchange(part, FAR).reshape(512, 128)
     p_mine = gather_near(part).reshape(HALF_P)

time: 130 us -> 127 us (0.977)
  blocking collectives: 81 us -> 55.1 us
  starting transfers between devices: 16.3 us -> 32.5 us
  waiting for transfers between devices: 14 us -> 20.7 us
    all_to_all x3 -> x2, blocking collectives: 58.5 us -> 33.2 us  [exchange(): lax.all_to_all(pieces, AXES, 0, 0, axis_index_groups=groups, tiled=True)]
    ppermute x0 -> x7, starting transfers between devices: none -> 13.3 us  [sum_near(): lax.ppermute(o, AXES, way_pairs(*way))]
    ppermute x0 -> x7, waiting for transfers between devices: none -> 8.66 us  [sum_near(): lax.ppermute(o, AXES, way_pairs(*way))]
    ppermute x7, waiting for transfers between devices: 10.7 us -> 8.92 us  [gather_near(): others = [lax.ppermute(block, AXES, way_pairs(*way)) for way in WAYS]]
    ppermute x7, starting transfers between devices: 7.16 us -> 8.63 us  [gather_near(): others = [lax.ppermute(block, AXES, way_pairs(*way)) for way in WAYS]]
    ppermute x6, starting transfers between devices: 9.15 us -> 10.6 us  [swap(): return lax.ppermute(value, axis, [(0, 1), (1, 0)])]
  transfers between devices with their start and end apart: 13 -> 20, of which waited for: 10 -> 11; matrix products, arithmetic and copies ran while one was open for 0% -> 0% of each run, Pallas kernels for 8% -> 8%
where the time goes in v1:
time: 127 us
  blocking collectives  55.1 us (43%)
  starting transfers between devices  32.5 us (26%)
  waiting for transfers between devices  20.7 us (16%)
  Pallas kernels  18 us (14%)
    all_to_all x2, blocking collectives, exchange(): lax.all_to_all(pieces, AXES, 0, 0, axis_index_groups=groups, tiled=True)  33.2 us
    ppermute x7, starting transfers between devices, sum_near(): lax.ppermute(o, AXES, way_pairs(*way))  13.3 us
    all_to_all x1, blocking collectives, per_device(): q_chips = lax.all_to_all(q_chips, 'z', 0, 0, tiled=True)  13.1 us
    ppermute x6, starting transfers between devices, swap(): return lax.ppermute(value, axis, [(0, 1), (1, 0)])  10.6 us
    ppermute x7, waiting for transfers between devices, gather_near(): others = [lax.ppermute(block, AXES, way_pairs(*way)) for way in WAYS]  8.92 us
    all_to_all x1, blocking collectives, per_device(): norm_parts = lax.all_to_all(norm_part[:, None], BLOCK, 0, 0, tiled=True)  8.71 us
    ppermute x7, waiting for transfers between devices, sum_near(): lax.ppermute(o, AXES, way_pairs(*way))  8.66 us
    ppermute x7, starting transfers between devices, gather_near(): others = [lax.ppermute(block, AXES, way_pairs(*way)) for way in WAYS]  8.63 us
  transfers between devices with their start and end apart: 20, of which 11 were waited for; matrix products, arithmetic and copies ran while one was open for 0% of the time, Pallas kernels for 8%

profile of v1, /device:TPU:1, one launch (start us, length us, event | category | flops | bytes accessed | tf_op | source)
XLA Modules:
  0.0 127.2 jit_solution(11543720900126122601)
XLA Ops:
  0.6 3.6 %left_half.3 = (f32[16,256,128]{2,1,0:T(8,128)S(1)}, bf16[16,512,128]{2,1,0:T(8,128)(2,1)S(1)}, bf16[16,512,128]{2,1,0:T(8,128)(2,1)S(1)}) custom-call(bf16[2,16,512,128]{3,2,1,0:T(8,128)(2,1)} %bitcast.37, bf16[2,16,512,128]{3,2,1,0:T(8,128)(2,1)} %bitcast.39, f32[128,128]{1,0:T(8,128)} %bitcast.41), custom_call_target="tpu_custom_call" | custom-call | flops 1073741824 | bytes 8388608 | tf_op jit(solution)/shard_map/left_half/pallas_call | solution.py:148
  4.2 3.3 %collective-permute-start = (f32[16,256,128]{2,1,0:T(8,128)S(1)}, f32[16,256,128]{2,1,0:T(8,128)S(1)}, u32[]{:S(2)}, u32[]{:S(2)}) collective-permute-start(f32[16,256,128]{2,1,0:T(8,128)S(1)} %get-tuple-element.30), channel_id=1, source_target_pairs={{0,8},{8,0},{1,9},{9,1},{2,10},{10,2},{3,11},{11,3},{4,12},{12,4},... | collective-permute-start | bytes 6291464 | tf_op jit(solution)/shard_map/ppermute | solution.py:509
  7.5 3.6 %left_half.2 = (f32[16,256,128]{2,1,0:T(8,128)S(1)}, bf16[16,512,128]{2,1,0:T(8,128)(2,1)S(1)}, bf16[16,512,128]{2,1,0:T(8,128)(2,1)S(1)}) custom-call(bf16[2,16,512,128]{3,2,1,0:T(8,128)(2,1)} %bitcast.38, bf16[2,16,512,128]{3,2,1,0:T(8,128)(2,1)} %bitcast.40, f32[128,128]{1,0:T(8,128)} %bitcast.42), custom_call_target="tpu_custom_call" | custom-call | flops 1073741824 | bytes 8388608 | tf_op jit(solution)/shard_map/left_half/pallas_call | solution.py:148
  11.1 0.2 collective-permute-done
  11.3 0.2 near_pieces.1
  11.5 3.9 %collective-permute-start.1 = (f32[512,128]{1,0:T(8,128)S(1)}, f32[512,128]{1,0:T(8,128)S(1)}, u32[]{:S(2)}, u32[]{:S(2)}) collective-permute-start(f32[512,128]{1,0:T(8,128)S(1)} %get-tuple-element.32), channel_id=1, source_target_pairs={{0,16},{1,17},{128,144},{129,145},{16,0},{17,1},{144,128},{145,129... | collective-permute-start | bytes 786440 | tf_op jit(solution)/shard_map/ppermute | solution.py:480
  15.5 1.3 %collective-permute-start.2 = (f32[512,128]{1,0:T(8,128)S(1)}, f32[512,128]{1,0:T(8,128)S(1)}, u32[]{:S(2)}, u32[]{:S(2)}) collective-permute-start(f32[512,128]{1,0:T(8,128)S(1)} %get-tuple-element.33), channel_id=1, source_target_pairs={{0,1},{1,128},{128,129},{129,0},{16,17},{17,144},{144,145},{145,16... | collective-permute-start | bytes 786440 | tf_op jit(solution)/shard_map/ppermute | solution.py:480
  16.7 1.4 %collective-permute-start.3 = (f32[512,128]{1,0:T(8,128)S(1)}, f32[512,128]{1,0:T(8,128)S(1)}, u32[]{:S(2)}, u32[]{:S(2)}) collective-permute-start(f32[512,128]{1,0:T(8,128)S(1)} %get-tuple-element.34), channel_id=1, source_target_pairs={{0,129},{1,0},{128,1},{129,128},{16,145},{17,16},{144,17},{145,144... | collective-permute-start | bytes 786440 | tf_op jit(solution)/shard_map/ppermute | solution.py:480
  18.2 1.6 %collective-permute-start.4 = (f32[512,128]{1,0:T(8,128)S(1)}, f32[512,128]{1,0:T(8,128)S(1)}, u32[]{:S(2)}, u32[]{:S(2)}) collective-permute-start(f32[512,128]{1,0:T(8,128)S(1)} %get-tuple-element.35), channel_id=1, source_target_pairs={{0,128},{1,129},{128,0},{129,1},{16,144},{17,145},{144,16},{145,17... | collective-permute-start | bytes 786440 | tf_op jit(solution)/shard_map/ppermute | solution.py:480
  19.8 0.2 collective-permute-start.5
  20.0 4.6 %collective-permute-start.6 = (f32[512,128]{1,0:T(8,128)S(1)}, f32[512,128]{1,0:T(8,128)S(1)}, u32[]{:S(2)}, u32[]{:S(2)}) collective-permute-start(f32[512,128]{1,0:T(8,128)S(1)} %get-tuple-element.37), channel_id=1, source_target_pairs={{0,145},{1,16},{128,17},{129,144},{16,129},{17,0},{144,1},{145,128... | collective-permute-start | bytes 786440 | tf_op jit(solution)/shard_map/ppermute | solution.py:480
  24.6 0.2 collective-permute-start.7
  24.8 4.5 %collective-permute-done.4.refs_4_ = f32[512,128]{1,0:T(8,128)S(1)} collective-permute-done((f32[512,128]{1,0:T(8,128)S(1)}, f32[512,128]{1,0:T(8,128)S(1)}, u32[]{:S(2)}, u32[]{:S(2)}) %collective-permute-start.4) | collective-permute-done | bytes 262176 | tf_op jit(solution)/shard_map/ppermute | solution.py:480
  29.4 0.0 collective-permute-done.5.refs_5_
  29.4 1.0 collective-permute-done.6.refs_6_
  30.3 3.1 %collective-permute-done.7.refs_7_ = f32[512,128]{1,0:T(8,128)S(1)} collective-permute-done((f32[512,128]{1,0:T(8,128)S(1)}, f32[512,128]{1,0:T(8,128)S(1)}, u32[]{:S(2)}, u32[]{:S(2)}) %collective-permute-start.7) | collective-permute-done | bytes 262176 | tf_op jit(solution)/shard_map/ppermute | solution.py:480
  33.5 0.1 sum_near.1
  33.6 17.4 %all_to_all.20.pieces = f32[16,32,128]{2,1,0:T(8,128)S(1)} all-to-all(f32[16,32,128]{2,1,0:T(8,128)S(1)} %bitcast.34), channel_id=1, replica_groups={{0,2,4,6,32,34,36,38,64,66,68,70,96,98,100,102},{16,18,20,22,48,50,52,5..., dimensions={0} | all-to-all | bytes 524288 | tf_op jit(solution)/shard_map/all_to_all | solution.py:68
  51.0 15.8 %all_to_all.21 = f32[16,32,128]{2,1,0:T(8,128)S(1)} all-to-all(f32[16,32,128]{2,1,0:T(8,128)S(1)} %sum_pieces.1), channel_id=1, replica_groups={{0,2,4,6,32,34,36,38,64,66,68,70,96,98,100,102},{16,18,20,22,48,50,52,5..., dimensions={0} | all-to-all | bytes 524288 | tf_op jit(solution)/shard_map/all_to_all | solution.py:68
  66.8 3.2 %collective-permute-start.13 = (f32[512,128]{1,0:T(8,128)S(1)}, f32[512,128]{1,0:T(8,128)S(1)}, u32[]{:S(2)}, u32[]{:S(2)}) collective-permute-start(f32[512,128]{1,0:T(8,128)S(1)} %bitcast.27), channel_id=1, source_target_pairs={{0,145},{1,16},{128,17},{129,144},{16,129},{17,0},{144,1},{145,128... | collective-permute-start | bytes 786440 | tf_op jit(solution)/shard_map/ppermute | solution.py:441
  70.1 0.3 collective-permute-start.12
  70.4 0.9 collective-permute-start.11
  71.3 2.7 %collective-permute-start.10 = (f32[512,128]{1,0:T(8,128)S(1)}, f32[512,128]{1,0:T(8,128)S(1)}, u32[]{:S(2)}, u32[]{:S(2)}) collective-permute-start(f32[512,128]{1,0:T(8,128)S(1)} %bitcast.30), channel_id=1, source_target_pairs={{0,129},{1,0},{128,1},{129,128},{16,145},{17,16},{144,17},{145,144... | collective-permute-start | bytes 786440 | tf_op jit(solution)/shard_map/ppermute | solution.py:441
  74.0 1.8 %collective-permute-done.14.rest_6_ = f32[512,128]{1,0:T(8,128)S(1)} collective-permute-done((f32[512,128]{1,0:T(8,128)S(1)}, f32[512,128]{1,0:T(8,128)S(1)}, u32[]{:S(2)}, u32[]{:S(2)}) %collective-permute-start.14) | collective-permute-done | bytes 262176 | tf_op jit(solution)/shard_map/ppermute | solution.py:441
  75.8 0.0 collective-permute-start.9
  75.8 0.0 collective-permute-done.13.rest_5_
  75.8 1.5 %collective-permute-start.8 = (f32[512,128]{1,0:T(8,128)S(1)}, f32[512,128]{1,0:T(8,128)S(1)}, u32[]{:S(2)}, u32[]{:S(2)}) collective-permute-start(f32[512,128]{1,0:T(8,128)S(1)} %bitcast.32), channel_id=1, source_target_pairs={{0,16},{1,17},{128,144},{129,145},{16,0},{17,1},{144,128},{145,129... | collective-permute-start | bytes 786440 | tf_op jit(solution)/shard_map/ppermute | solution.py:441
  77.2 3.9 %collective-permute-done.12.rest_4_ = f32[512,128]{1,0:T(8,128)S(1)} collective-permute-done((f32[512,128]{1,0:T(8,128)S(1)}, f32[512,128]{1,0:T(8,128)S(1)}, u32[]{:S(2)}, u32[]{:S(2)}) %collective-permute-start.12) | collective-permute-done | bytes 262176 | tf_op jit(solution)/shard_map/ppermute | solution.py:441
  81.1 0.9 collective-permute-done.11.rest_3_
  82.0 0.0 collective-permute-done.10.rest_2_
  82.0 2.4 %collective-permute-done.9.rest_1_ = f32[512,128]{1,0:T(8,128)S(1)} collective-permute-done((f32[512,128]{1,0:T(8,128)S(1)}, f32[512,128]{1,0:T(8,128)S(1)}, u32[]{:S(2)}, u32[]{:S(2)}) %collective-permute-start.9) | collective-permute-done | bytes 262176 | tf_op jit(solution)/shard_map/ppermute | solution.py:441
  84.4 0.2 gather_near.1
  84.5 2.2 %collective-permute-start.16 = (f32[16,256,128]{2,1,0:T(8,128)S(1)}, f32[16,256,128]{2,1,0:T(8,128)S(1)}, u32[]{:S(2)}, u32[]{:S(2)}) collective-permute-start(f32[16,256,128]{2,1,0:T(8,128)S(1)} %bitcast.21), channel_id=1, source_target_pairs={{0,8},{8,0},{1,9},{9,1},{2,10},{10,2},{3,11},{11,3},{4,12},{12,4},... | collective-permute-start | bytes 6291464 | tf_op jit(solution)/shard_map/ppermute | solution.py:509
  86.8 2.2 %right_half.1 = (f32[128,128]{1,0:T(8,128)S(1)}, f32[128,128]{1,0:T(8,128)S(1)}, bf16[16,512,256]{2,1,0:T(8,128)(2,1)S(1)}) custom-call(f32[16,256,128]{2,1,0:T(8,128)S(1)} %bitcast.22, bf16[16,512,128]{2,1,0:T(8,128)(2,1)S(1)} %get-tuple-element.39.g_ref.rest_1_, bf16[16,512,128]{2,1,0:T(8,128)(2,1)S(1)} %get-tuple-element.40.e_ref.rest_2_), custom_call_target="tpu_custom_call" | custom-call | flops 1610612736 | bytes 6291456 | tf_op jit(solution)/shard_map/right_half/pallas_call | solution.py:219
  89.0 0.1 collective-permute-start.15
  89.1 1.4 %collective-permute-done.16.p_ref.p_other = f32[16,256,128]{2,1,0:T(8,128)S(1)} collective-permute-done((f32[16,256,128]{2,1,0:T(8,128)S(1)}, f32[16,256,128]{2,1,0:T(8,128)S(1)}, u32[]{:S(2)}, u32[]{:S(2)}) %collective-permute-start.16) | collective-permute-done | bytes 2097184 | tf_op jit(solution)/shard_map/ppermute | solution.py:509
  90.6 1.8 %other_half.1 = (f32[64,128]{1,0:T(8,128)S(1)}, f32[64,128]{1,0:T(8,128)S(1)}, bf16[16,512,256]{2,1,0:T(8,128)(2,1)S(1)}) custom-call(f32[16,256,128]{2,1,0:T(8,128)S(1)} %collective-permute-done.16.p_ref.p_other, bf16[16,512,128]{2,1,0:T(8,128)(2,1)S(1)} %get-tuple-element.42.g_ref.rest_4_, bf16[16,512,128]{2,1,0:T(8,128)(2,1)S(1)} %get-tuple-element.43.e_ref.rest_5_, ...), custom_call_target="tpu_custom_call" | custom-call | flops 1073741824 | bytes 6291456 | tf_op jit(solution)/shard_map/other_half/pallas_call | solution.py:286
  92.4 0.5 collective-permute-start.17
  92.8 0.9 collective-permute-done.17
  93.7 1.1 collective-permute-start.18
  94.8 0.0 collective-permute-done.15.gram_other
  94.8 2.5 %solve.1 = (f32[128,128]{1,0:T(8,128)S(1)}, bf16[128,256]{1,0:T(8,128)(2,1)}) custom-call(f32[128,128]{1,0:T(8,128)S(1)} %get-tuple-element.41.gram_in, f32[128,128]{1,0:T(8,128)S(1)} %collective-permute-done.15.gram_other, f32[16,256,128]{2,1,0:T(8,128)S(1)} %bitcast.23, f32[16,256,128]{2,1,0:T(8,128)S(1)} %collective-permute-done.16.p_ref.p_other, ...), custom_call_target="tpu_custom_call" | custom-call | flops 1073741824 | bytes 1048576 | tf_op jit(solution)/shard_map/solve/pallas_call | solution.py:312
  97.3 0.6 collective-permute-done.18.b_ref
  98.0 13.1 %all_to_all.22.pieces = f32[8,64,128]{2,1,0:T(8,128)S(1)} all-to-all(f32[8,64,128]{2,1,0:T(8,128)S(1)} %add_for_each.1), channel_id=1, replica_groups=mesh['x_hi'=2,'z'=8,'core'=2,'y'=4,'x_lo'=2] {'z'}, dimensions={0} | all-to-all | bytes 524288 | tf_op jit(solution)/shard_map/all_to_all | solution.py:534
  111.1 0.3 mean.1
  111.4 3.4 %collective-permute-start.19 = (f32[64,128]{1,0:T(8,128)S(1)}, f32[64,128]{1,0:T(8,128)S(1)}, u32[]{:S(2)}, u32[]{:S(2)}) collective-permute-start(f32[64,128]{1,0:T(8,128)S(1)} %get-tuple-element.48.q_mine), channel_id=1, source_target_pairs={{0,8},{8,0},{1,9},{9,1},{2,10},{10,2},{3,11},{11,3},{4,12},{12,4},... | collective-permute-start | bytes 98312 | tf_op jit(solution)/shard_map/ppermute | solution.py:509
  114.8 8.7 %all_to_all.23 = f32[16,1,128]{2,1,0:T(1,128)S(1)} all-to-all(f32[16,1,128]{2,1,0:T(1,128)S(1)} %bitcast.36), channel_id=1, replica_groups=mesh['x_hi'=2,'z'=8,'core'=2,'y'=4,'x_lo'=2] {'core','y','x_lo'}, dimensions={0} | all-to-all | bytes 16384 | tf_op jit(solution)/shard_map/all_to_all | solution.py:537
  123.5 3.5 %new_errors.1 = (bf16[2,16,512,128]{3,2,1,0:T(8,128)(2,1)}, f32[128,128]{1,0:T(8,128)}) custom-call(f32[128,128]{1,0:T(8,128)S(1)} %get-tuple-element.47.after.inverse_ref, f32[64,128]{1,0:T(8,128)S(1)} %get-tuple-element.48.q_mine, f32[64,128]{1,0:T(8,128)S(1)} %collective-permute-done.19.q_other, f32[16,128]{1,0:T(8,128)S(1)} %bitcast.35, ...), custom_call_target="tpu_custom_call" | custom-call | flops 2147483648 | bytes 16777216 | tf_op jit(solution)/shard_map/new_errors/pallas_call | solution.py:384
  (9 shorter events, 0.1 us)
Async XLA Ops:
  4.2 7.1 %collective-permute-start = (f32[16,256,128]{2,1,0:T(8,128)S(1)}, f32[16,256,128]{2,1,0:T(8,128)S(1)}, u32[]{:S(2)}, u32[]{:S(2)}) collective-permute-start(f32[16,256,128]{2,1,0:T(8,128)S(1)} %get-tuple-element.30), channel_id=1, source_target_pairs={{0,8},{8,0},{1,9},{9,1},{2,10},{10,2},{3,11},{11,3},{4,12},{12,4},... | collective-permute-start | bytes 6291464 | tf_op jit(solution)/shard_map/ppermute | solution.py:509
  11.5 8.5 %collective-permute-start.1 = (f32[512,128]{1,0:T(8,128)S(1)}, f32[512,128]{1,0:T(8,128)S(1)}, u32[]{:S(2)}, u32[]{:S(2)}) collective-permute-start(f32[512,128]{1,0:T(8,128)S(1)} %get-tuple-element.32), channel_id=1, source_target_pairs={{0,16},{1,17},{128,144},{129,145},{16,0},{17,1},{144,128},{145,129... | collective-permute-start | bytes 786440 | tf_op jit(solution)/shard_map/ppermute | solution.py:480
  15.5 9.2 %collective-permute-start.2 = (f32[512,128]{1,0:T(8,128)S(1)}, f32[512,128]{1,0:T(8,128)S(1)}, u32[]{:S(2)}, u32[]{:S(2)}) collective-permute-start(f32[512,128]{1,0:T(8,128)S(1)} %get-tuple-element.33), channel_id=1, source_target_pairs={{0,1},{1,128},{128,129},{129,0},{16,17},{17,144},{144,145},{145,16... | collective-permute-start | bytes 786440 | tf_op jit(solution)/shard_map/ppermute | solution.py:480
  16.7 8.1 %collective-permute-start.3 = (f32[512,128]{1,0:T(8,128)S(1)}, f32[512,128]{1,0:T(8,128)S(1)}, u32[]{:S(2)}, u32[]{:S(2)}) collective-permute-start(f32[512,128]{1,0:T(8,128)S(1)} %get-tuple-element.34), channel_id=1, source_target_pairs={{0,129},{1,0},{128,1},{129,128},{16,145},{17,16},{144,17},{145,144... | collective-permute-start | bytes 786440 | tf_op jit(solution)/shard_map/ppermute | solution.py:480
  18.2 11.2 %collective-permute-start.4 = (f32[512,128]{1,0:T(8,128)S(1)}, f32[512,128]{1,0:T(8,128)S(1)}, u32[]{:S(2)}, u32[]{:S(2)}) collective-permute-start(f32[512,128]{1,0:T(8,128)S(1)} %get-tuple-element.35), channel_id=1, source_target_pairs={{0,128},{1,129},{128,0},{129,1},{16,144},{17,145},{144,16},{145,17... | collective-permute-start | bytes 786440 | tf_op jit(solution)/shard_map/ppermute | solution.py:480
  19.8 9.5 %collective-permute-start.5 = (f32[512,128]{1,0:T(8,128)S(1)}, f32[512,128]{1,0:T(8,128)S(1)}, u32[]{:S(2)}, u32[]{:S(2)}) collective-permute-start(f32[512,128]{1,0:T(8,128)S(1)} %get-tuple-element.36), channel_id=1, source_target_pairs={{0,17},{1,144},{128,145},{129,16},{16,1},{17,128},{144,129},{145,0... | collective-permute-start | bytes 786440 | tf_op jit(solution)/shard_map/ppermute | solution.py:480
  20.0 10.3 %collective-permute-start.6 = (f32[512,128]{1,0:T(8,128)S(1)}, f32[512,128]{1,0:T(8,128)S(1)}, u32[]{:S(2)}, u32[]{:S(2)}) collective-permute-start(f32[512,128]{1,0:T(8,128)S(1)} %get-tuple-element.37), channel_id=1, source_target_pairs={{0,145},{1,16},{128,17},{129,144},{16,129},{17,0},{144,1},{145,128... | collective-permute-start | bytes 786440 | tf_op jit(solution)/shard_map/ppermute | solution.py:480
  24.6 8.8 %collective-permute-start.7 = (f32[512,128]{1,0:T(8,128)S(1)}, f32[512,128]{1,0:T(8,128)S(1)}, u32[]{:S(2)}, u32[]{:S(2)}) collective-permute-start(f32[512,128]{1,0:T(8,128)S(1)} %get-tuple-element.38), channel_id=1, source_target_pairs={{0,144},{1,145},{128,16},{129,17},{16,128},{17,129},{144,0},{145,1... | collective-permute-start | bytes 786440 | tf_op jit(solution)/shard_map/ppermute | solution.py:480
  66.8 8.9 %collective-permute-start.14 = (f32[512,128]{1,0:T(8,128)S(1)}, f32[512,128]{1,0:T(8,128)S(1)}, u32[]{:S(2)}, u32[]{:S(2)}) collective-permute-start(f32[512,128]{1,0:T(8,128)S(1)} %bitcast.26), channel_id=1, source_target_pairs={{0,144},{1,145},{128,16},{129,17},{16,128},{17,129},{144,0},{145,1... | collective-permute-start | bytes 786440 | tf_op jit(solution)/shard_map/ppermute | solution.py:441
  66.8 8.9 %collective-permute-start.13 = (f32[512,128]{1,0:T(8,128)S(1)}, f32[512,128]{1,0:T(8,128)S(1)}, u32[]{:S(2)}, u32[]{:S(2)}) collective-permute-start(f32[512,128]{1,0:T(8,128)S(1)} %bitcast.27), channel_id=1, source_target_pairs={{0,145},{1,16},{128,17},{129,144},{16,129},{17,0},{144,1},{145,128... | collective-permute-start | bytes 786440 | tf_op jit(solution)/shard_map/ppermute | solution.py:441
  70.1 11.0 %collective-permute-start.12 = (f32[512,128]{1,0:T(8,128)S(1)}, f32[512,128]{1,0:T(8,128)S(1)}, u32[]{:S(2)}, u32[]{:S(2)}) collective-permute-start(f32[512,128]{1,0:T(8,128)S(1)} %bitcast.28), channel_id=1, source_target_pairs={{0,17},{1,144},{128,145},{129,16},{16,1},{17,128},{144,129},{145,0... | collective-permute-start | bytes 786440 | tf_op jit(solution)/shard_map/ppermute | solution.py:441
  70.4 11.6 %collective-permute-start.11 = (f32[512,128]{1,0:T(8,128)S(1)}, f32[512,128]{1,0:T(8,128)S(1)}, u32[]{:S(2)}, u32[]{:S(2)}) collective-permute-start(f32[512,128]{1,0:T(8,128)S(1)} %bitcast.29), channel_id=1, source_target_pairs={{0,128},{1,129},{128,0},{129,1},{16,144},{17,145},{144,16},{145,17... | collective-permute-start | bytes 786440 | tf_op jit(solution)/shard_map/ppermute | solution.py:441
  71.3 10.8 %collective-permute-start.10 = (f32[512,128]{1,0:T(8,128)S(1)}, f32[512,128]{1,0:T(8,128)S(1)}, u32[]{:S(2)}, u32[]{:S(2)}) collective-permute-start(f32[512,128]{1,0:T(8,128)S(1)} %bitcast.30), channel_id=1, source_target_pairs={{0,129},{1,0},{128,1},{129,128},{16,145},{17,16},{144,17},{145,144... | collective-permute-start | bytes 786440 | tf_op jit(solution)/shard_map/ppermute | solution.py:441
  75.8 8.6 %collective-permute-start.9 = (f32[512,128]{1,0:T(8,128)S(1)}, f32[512,128]{1,0:T(8,128)S(1)}, u32[]{:S(2)}, u32[]{:S(2)}) collective-permute-start(f32[512,128]{1,0:T(8,128)S(1)} %bitcast.31), channel_id=1, source_target_pairs={{0,1},{1,128},{128,129},{129,0},{16,17},{17,144},{144,145},{145,16... | collective-permute-start | bytes 786440 | tf_op jit(solution)/shard_map/ppermute | solution.py:441
  75.8 8.6 %collective-permute-start.8 = (f32[512,128]{1,0:T(8,128)S(1)}, f32[512,128]{1,0:T(8,128)S(1)}, u32[]{:S(2)}, u32[]{:S(2)}) collective-permute-start(f32[512,128]{1,0:T(8,128)S(1)} %bitcast.32), channel_id=1, source_target_pairs={{0,16},{1,17},{128,144},{129,145},{16,0},{17,1},{144,128},{145,129... | collective-permute-start | bytes 786440 | tf_op jit(solution)/shard_map/ppermute | solution.py:441
  84.5 6.0 %collective-permute-start.16 = (f32[16,256,128]{2,1,0:T(8,128)S(1)}, f32[16,256,128]{2,1,0:T(8,128)S(1)}, u32[]{:S(2)}, u32[]{:S(2)}) collective-permute-start(f32[16,256,128]{2,1,0:T(8,128)S(1)} %bitcast.21), channel_id=1, source_target_pairs={{0,8},{8,0},{1,9},{9,1},{2,10},{10,2},{3,11},{11,3},{4,12},{12,4},... | collective-permute-start | bytes 6291464 | tf_op jit(solution)/shard_map/ppermute | solution.py:509
  89.0 5.8 %collective-permute-start.15 = (f32[128,128]{1,0:T(8,128)S(1)}, f32[128,128]{1,0:T(8,128)S(1)}, u32[]{:S(2)}, u32[]{:S(2)}) collective-permute-start(f32[128,128]{1,0:T(8,128)S(1)} %get-tuple-element.41.gram_in), channel_id=1, source_target_pairs={{0,8},{8,0},{1,9},{9,1},{2,10},{10,2},{3,11},{11,3},{4,12},{12,4},... | collective-permute-start | bytes 196616 | tf_op jit(solution)/shard_map/ppermute | solution.py:509
  92.4 1.3 %collective-permute-start.17 = (f32[64,128]{1,0:T(8,128)S(1)}, f32[64,128]{1,0:T(8,128)S(1)}, u32[]{:S(2)}, u32[]{:S(2)}) collective-permute-start(f32[64,128]{1,0:T(8,128)S(1)} %get-tuple-element.46), channel_id=1, source_target_pairs={{0,8},{8,0},{1,9},{9,1},{2,10},{10,2},{3,11},{11,3},{4,12},{12,4},... | collective-permute-start | bytes 98312 | tf_op jit(solution)/shard_map/ppermute | solution.py:509
  93.7 4.3 %collective-permute-start.18 = (f32[64,128]{1,0:T(8,128)S(1)}, f32[64,128]{1,0:T(8,128)S(1)}, u32[]{:S(2)}, u32[]{:S(2)}) collective-permute-start(f32[64,128]{1,0:T(8,128)S(1)} %add.3.after.a_ref), channel_id=1, source_target_pairs={{0,128},{128,0},{1,129},{129,1},{2,130},{130,2},{3,131},{131,3},{4... | collective-permute-start | bytes 98312 | tf_op jit(solution)/shard_map/ppermute | solution.py:509
  111.4 12.1 %collective-permute-start.19 = (f32[64,128]{1,0:T(8,128)S(1)}, f32[64,128]{1,0:T(8,128)S(1)}, u32[]{:S(2)}, u32[]{:S(2)}) collective-permute-start(f32[64,128]{1,0:T(8,128)S(1)} %get-tuple-element.48.q_mine), channel_id=1, source_target_pairs={{0,8},{8,0},{1,9},{9,1},{2,10},{10,2},{3,11},{11,3},{4,12},{12,4},... | collective-permute-start | bytes 98312 | tf_op jit(solution)/shard_map/ppermute | solution.py:509
